TPU v7x, 32 devices: a whole 2x2x4 slice. The times are simulated.
32 devices in a mesh: seq: 2 (over x), ctx: 16 (over z, y, core).
Axes of the slice: x: 2, y: 2, z: 4, core: 2. Of those that a mesh axis runs over, the one named last changes fastest.
Arguments:
- tokens: bfloat16 [2, 2048, 2048], P('seq', 'ctx'), may hold values from -80 to 80
- qkv_weight: bfloat16 [2048, 1536], P(None, 'seq'), may hold values from -0.125 to 0.125
- doc_lengths: int32 [2, 12], P('seq'), may hold values from 1 to 256, 2048 in all within a row
- span_order: int32 [2, 32], P('seq'), may hold values from 0 to 31, as said below
Outputs:
- attended: bfloat16 [2, 2048, 1024], P('seq', 'ctx')
Inputs may be any that keep to these rules, and one draw needn't show every extreme that they name: `doc_lengths`: each row sums to 2048; its largest entry is exactly 256. `span_order`: in each row, slots 2 i and 2 i + 1 hold spans i and 31 - i, in an order drawn for each pair.
All inputs are finite; a program needn't handle non-finite values.
Results may differ from a plain program's by a relative error of at most 0.012.
The roundings to bfloat16 on the way count: a program that leaves them out, or rounds other values in their place, can miss the bound.
Values may be sent and summed in bfloat16 or wider, within the bound.
A program may use at most 192 MiB of HBM per device.

v0:
```python
import jax
import jax.numpy as jnp
from jax import lax
from jax.sharding import PartitionSpec as P

QUERY_HEADS = 16
KEY_VALUE_HEADS = 4
HEAD_SIZE = 64
QUERY_PER_KV = 4
SPAN = 64


def shifted(value, axis, steps):
    count = lax.axis_size(axis)
    initial, last = (max(0, -steps), min(count, count - steps))
    return lax.ppermute(value, axis, [(source, source + steps) for source in range(initial, last)])


def apply_rotary(value_rows, token_positions):
    token_count = value_rows.shape[0]
    heads = value_rows.reshape(token_count, -1, HEAD_SIZE)
    half = HEAD_SIZE // 2
    freq = 500000.0 ** (-jnp.arange(half, dtype=jnp.float32) * 2.0 / HEAD_SIZE)
    angle = token_positions.astype(jnp.float32)[:, None] * freq[None, :]
    cosine = jnp.cos(angle)[:, None, :]
    sine = jnp.sin(angle)[:, None, :]
    first = heads[..., :half]
    second = heads[..., half:]
    turned = jnp.concatenate(
        [first * cosine - second * sine, second * cosine + first * sine], axis=-1
    )
    return turned.reshape(token_count, -1)


def positions(order_row):
    offsets = jnp.arange(SPAN, dtype=jnp.int32)
    return (order_row[:, None] * SPAN + offsets[None, :]).reshape(-1)


def documents(lengths_row, token_positions):
    ends = jnp.cumsum(lengths_row)
    return jnp.sum((ends[None, :] <= token_positions[:, None]).astype(jnp.int32), axis=1)


def body(tokens, qkv_weight, doc_lengths, span_order):
    rows = tokens[0]
    token_count = rows.shape[0]
    query_key_value = jnp.dot(
        rows,
        lax.all_gather(qkv_weight, "seq", axis=1, tiled=True),
        preferred_element_type=jnp.float32,
    ).astype(jnp.bfloat16)
    lengths_row = doc_lengths[0]
    order_row = span_order[0]
    places_all = positions(order_row)
    docs_all = documents(lengths_row, places_all)
    my_index = lax.axis_index("ctx")
    first_row = my_index * token_count
    token_positions = lax.dynamic_slice_in_dim(places_all, first_row, token_count)
    docs = lax.dynamic_slice_in_dim(docs_all, first_row, token_count)
    query_rows = apply_rotary(
        query_key_value[:, : QUERY_HEADS * HEAD_SIZE].astype(jnp.float32), token_positions
    ).astype(jnp.bfloat16)
    key_rows = apply_rotary(
        query_key_value[
            :, QUERY_HEADS * HEAD_SIZE : (QUERY_HEADS + KEY_VALUE_HEADS) * HEAD_SIZE
        ].astype(jnp.float32),
        token_positions,
    ).astype(jnp.bfloat16)
    value_rows = query_key_value[:, (QUERY_HEADS + KEY_VALUE_HEADS) * HEAD_SIZE :]
    query_head_rows = query_rows.reshape(token_count, KEY_VALUE_HEADS, QUERY_PER_KV, HEAD_SIZE)

    def absorb_block(carry, key_block_part, value_block_part, key_places, key_docs, usable):
        block_rows = key_block_part.shape[0]
        live = (
            (docs[:, None] == key_docs[None, :])
            & (key_places[None, :] <= token_positions[:, None])
            & usable
        )
        running_state, total, summed = carry
        key_head_rows = key_block_part.reshape(block_rows, KEY_VALUE_HEADS, HEAD_SIZE)
        value_head_rows = value_block_part.reshape(block_rows, KEY_VALUE_HEADS, HEAD_SIZE)
        scores = (
            jnp.einsum(
                "qhgd,khd->hgqk", query_head_rows, key_head_rows, preferred_element_type=jnp.float32
            )
            * 0.125
        )
        scores = jnp.where(live, scores, -1e30)
        newest = jnp.maximum(running_state, jnp.max(scores, axis=-1))
        factor = jnp.exp(running_state - newest)
        weights = jnp.where(live, jnp.exp(scores - newest[..., None]), 0.0)
        total = total * factor + jnp.sum(weights, axis=-1)
        added = jnp.einsum(
            "hgqk,khd->hgqd",
            weights.astype(jnp.bfloat16),
            value_head_rows,
            preferred_element_type=jnp.float32,
        )
        summed = summed * factor[..., None] + added
        return (newest, total, summed)

    initial = (
        jnp.full((KEY_VALUE_HEADS, QUERY_PER_KV, token_count), -1e30, jnp.float32),
        jnp.zeros((KEY_VALUE_HEADS, QUERY_PER_KV, token_count), jnp.float32),
        jnp.zeros((KEY_VALUE_HEADS, QUERY_PER_KV, token_count, HEAD_SIZE), jnp.float32),
    )
    devices = lax.axis_size("ctx")
    key_cols = key_rows.shape[1]
    stacked = jnp.concatenate([key_rows, value_rows], axis=1)
    early_first = order_row[2 * my_index] < devices
    offset = jnp.where(early_first, 0, SPAN).astype(jnp.int32)
    early_rows = lax.dynamic_slice_in_dim(stacked, offset, SPAN, 0)
    late_rows = lax.dynamic_slice_in_dim(stacked, SPAN - offset, SPAN, 0)
    pair_rows = jnp.concatenate([early_rows, late_rows], axis=0)
    ramp = jnp.arange(SPAN, dtype=jnp.int32)
    state = absorb_block(initial, key_rows, value_rows, token_positions, docs, jnp.array(True))

    def advance(step, loop_state):
        carry, upward, downward = loop_state
        upward = shifted(upward, "ctx", 1)
        downward = shifted(downward, "ctx", -1)
        lower = my_index - step
        upper = my_index + step
        up_places = lower * SPAN + ramp
        carry = absorb_block(
            carry,
            upward[:, :key_cols],
            upward[:, key_cols:],
            up_places,
            documents(lengths_row, up_places),
            lower >= 0,
        )
        down_places = jnp.concatenate(
            [upper * SPAN + ramp, (2 * devices - 1 - upper) * SPAN + ramp]
        )
        carry = absorb_block(
            carry,
            downward[:, :key_cols],
            downward[:, key_cols:],
            down_places,
            documents(lengths_row, down_places),
            upper < devices,
        )
        return (carry, upward, downward)

    final_state = lax.fori_loop(1, devices // 4 + 1, advance, (state, early_rows, pair_rows))
    running_state, total, summed = final_state[0]
    outputs = summed / total[..., None]
    outputs = (
        jnp.transpose(outputs, (2, 0, 1, 3))
        .reshape(token_count, QUERY_HEADS * HEAD_SIZE)
        .astype(jnp.bfloat16)
    )
    return outputs[None]


def solution(mesh):
    placed = (P("seq", "ctx", None), P(None, "seq"), P("seq", None), P("seq", None))
    return jax.shard_map(
        body, mesh=mesh, in_specs=placed, out_specs=P("seq", "ctx", None), check_vma=False
    )
```

profile of v0, /device:TPU:8, one launch (start us, length us, event | category | flops | bytes accessed | tf_op | source)
XLA Modules:
  0.0 145.7 jit_solution(8218920867855288570)
XLA Ops:
  6.5 0.7 all-gather.2.cloned.1.call-update
  7.3 0.7 multiply_bitcast_fusion
  8.1 0.8 broadcast_in_dim.146
  8.9 0.8 reduce-window.9
  9.7 1.3 fusion.44
  12.1 0.1 multiply_cosine_fusion
  12.2 78.3 %all-gather.2.cloned.1.call-done = bf16[2048,1536]{1,0:T(8,128)(2,1)} async-done(((bf16[2048,768]{1,0:T(8,128)(2,1)}), bf16[2048,1536]{1,0:T(8,128)(2,1)}) %all-gather.2.cloned.1.call-update) | async-done | bytes 6291472 | tf_op jit(solution)/shard_map/all_gather | solution.py:50
  90.5 3.8 %convolution_convert_fusion = bf16[128,1536]{1,0:T(8,128)(2,1)S(1)} fusion(bf16[2048,1536]{1,0:T(8,128)(2,1)} %all-gather.2.cloned.1.call-done, bf16[1,128,2048]{2,1,0:T(8,128)(2,1)S(1)} %copy-done), kind=kOutput, calls=%fused_computation.36 | convolution fusion | flops 805502976 | bytes 7208960 | tf_op jit(solution)/shard_map/dot_general | solution.py:48
  94.4 0.2 copy.31
  94.8 0.4 fusion.43
  95.2 0.2 fusion.25
  95.8 0.3 convolution_add_fusion.2
  96.1 41.8 %while.25 = (s32[]{:T(128)}, f32[4,4,128]{2,1,0:T(4,128)S(1)}, f32[4,4,128]{2,1,0:T(4,128)S(1)}, f32[4,4,128,64]{2,3,1,0:T(8,128)S(1)}, bf16[64,512]{1,0:T(8,128...) while((s32[]{:T(128)}, f32[4,4,128]{2,1,0:T(4,128)S(1)}, ...), condition=%wide.region_12.13_spmd.clone.clone, body=%wide.region_5.12_spmd.clone.clone.sunk | while | flops 104840072 | bytes 9559213 | solution.py:147
  96.2 2.8 %collective-permute-start = (bf16[128,512]{0,1:T(8,128)(2,1)S(1)}, bf16[128,512]{0,1:T(8,128)(2,1)S(1)}, u32[]{:S(2)}, u32[]{:S(2)}) collective-permute-start(bf16[128,512]{0,1:T(8,128)(2,1)S(1)} %get-tuple-element.556), channel_id=1, source_target_pairs={{1,0},{2,1},{3,2},{4,3},{5,4},{6,5},{7,6},{8,7},{9,8},{10,9},{11,1... | collective-permute-start | bytes 393224 | tf_op jit(solution)/shard_map/while/body/eval_jaxpr/ppermute | solution.py:16
  99.0 1.9 %collective-permute-start.1 = (bf16[64,512]{1,0:T(8,128)(2,1)S(1)}, bf16[64,512]{1,0:T(8,128)(2,1)S(1)}, u32[]{:S(2)}, u32[]{:S(2)}) collective-permute-start(bf16[64,512]{1,0:T(8,128)(2,1)S(1)} %get-tuple-element.555), channel_id=1, source_target_pairs={{0,1},{1,2},{2,3},{3,4},{4,5},{5,6},{6,7},{7,8},{8,9},{9,10},{10,1... | collective-permute-start | bytes 196616 | tf_op jit(solution)/shard_map/while/body/eval_jaxpr/ppermute | solution.py:16
  101.4 4.1 %collective-permute-done.1 = bf16[64,512]{1,0:T(8,128)(2,1)S(1)} collective-permute-done((bf16[64,512]{1,0:T(8,128)(2,1)S(1)}, bf16[64,512]{1,0:T(8,128)(2,1)S(1)}, u32[]{:S(2)}, u32[]{:S(2)}) %collective-permute-start.1) | collective-permute-done | bytes 65568 | tf_op jit(solution)/shard_map/while/body/eval_jaxpr/ppermute | solution.py:16
  105.7 0.2 fusion.78
  106.0 0.4 fusion.76
  106.3 0.2 fusion.80
  106.5 0.1 fusion.81
  106.7 0.2 fusion.82
  106.9 0.3 convolution_add_fusion.4
  107.3 1.9 %collective-permute-start = (bf16[128,512]{0,1:T(8,128)(2,1)S(1)}, bf16[128,512]{0,1:T(8,128)(2,1)S(1)}, u32[]{:S(2)}, u32[]{:S(2)}) collective-permute-start(bf16[128,512]{0,1:T(8,128)(2,1)S(1)} %get-tuple-element.556), channel_id=1, source_target_pairs={{1,0},{2,1},{3,2},{4,3},{5,4},{6,5},{7,6},{8,7},{9,8},{10,9},{11,1... | collective-permute-start | bytes 393224 | tf_op jit(solution)/shard_map/while/body/eval_jaxpr/ppermute | solution.py:16
  109.2 2.4 %collective-permute-start.1 = (bf16[64,512]{1,0:T(8,128)(2,1)S(1)}, bf16[64,512]{1,0:T(8,128)(2,1)S(1)}, u32[]{:S(2)}, u32[]{:S(2)}) collective-permute-start(bf16[64,512]{1,0:T(8,128)(2,1)S(1)} %get-tuple-element.555), channel_id=1, source_target_pairs={{0,1},{1,2},{2,3},{3,4},{4,5},{5,6},{6,7},{7,8},{8,9},{9,10},{10,1... | collective-permute-start | bytes 196616 | tf_op jit(solution)/shard_map/while/body/eval_jaxpr/ppermute | solution.py:16
  112.1 3.6 %collective-permute-done.1 = bf16[64,512]{1,0:T(8,128)(2,1)S(1)} collective-permute-done((bf16[64,512]{1,0:T(8,128)(2,1)S(1)}, bf16[64,512]{1,0:T(8,128)(2,1)S(1)}, u32[]{:S(2)}, u32[]{:S(2)}) %collective-permute-start.1) | collective-permute-done | bytes 65568 | tf_op jit(solution)/shard_map/while/body/eval_jaxpr/ppermute | solution.py:16
  115.9 0.2 fusion.78
  116.2 0.4 fusion.76
  116.6 0.2 fusion.80
  116.8 0.1 fusion.81
  116.9 0.2 fusion.82
  117.2 0.3 convolution_add_fusion.4
  117.5 1.9 %collective-permute-start = (bf16[128,512]{0,1:T(8,128)(2,1)S(1)}, bf16[128,512]{0,1:T(8,128)(2,1)S(1)}, u32[]{:S(2)}, u32[]{:S(2)}) collective-permute-start(bf16[128,512]{0,1:T(8,128)(2,1)S(1)} %get-tuple-element.556), channel_id=1, source_target_pairs={{1,0},{2,1},{3,2},{4,3},{5,4},{6,5},{7,6},{8,7},{9,8},{10,9},{11,1... | collective-permute-start | bytes 393224 | tf_op jit(solution)/shard_map/while/body/eval_jaxpr/ppermute | solution.py:16
  119.4 2.4 %collective-permute-start.1 = (bf16[64,512]{1,0:T(8,128)(2,1)S(1)}, bf16[64,512]{1,0:T(8,128)(2,1)S(1)}, u32[]{:S(2)}, u32[]{:S(2)}) collective-permute-start(bf16[64,512]{1,0:T(8,128)(2,1)S(1)} %get-tuple-element.555), channel_id=1, source_target_pairs={{0,1},{1,2},{2,3},{3,4},{4,5},{5,6},{6,7},{7,8},{8,9},{9,10},{10,1... | collective-permute-start | bytes 196616 | tf_op jit(solution)/shard_map/while/body/eval_jaxpr/ppermute | solution.py:16
  122.3 3.6 %collective-permute-done.1 = bf16[64,512]{1,0:T(8,128)(2,1)S(1)} collective-permute-done((bf16[64,512]{1,0:T(8,128)(2,1)S(1)}, bf16[64,512]{1,0:T(8,128)(2,1)S(1)}, u32[]{:S(2)}, u32[]{:S(2)}) %collective-permute-start.1) | collective-permute-done | bytes 65568 | tf_op jit(solution)/shard_map/while/body/eval_jaxpr/ppermute | solution.py:16
  126.2 0.2 fusion.78
  126.4 0.4 fusion.76
  126.8 0.2 fusion.80
  127.2 0.2 fusion.82
  127.4 0.3 convolution_add_fusion.4
  127.7 1.9 %collective-permute-start = (bf16[128,512]{0,1:T(8,128)(2,1)S(1)}, bf16[128,512]{0,1:T(8,128)(2,1)S(1)}, u32[]{:S(2)}, u32[]{:S(2)}) collective-permute-start(bf16[128,512]{0,1:T(8,128)(2,1)S(1)} %get-tuple-element.556), channel_id=1, source_target_pairs={{1,0},{2,1},{3,2},{4,3},{5,4},{6,5},{7,6},{8,7},{9,8},{10,9},{11,1... | collective-permute-start | bytes 393224 | tf_op jit(solution)/shard_map/while/body/eval_jaxpr/ppermute | solution.py:16
  129.7 2.4 %collective-permute-start.1 = (bf16[64,512]{1,0:T(8,128)(2,1)S(1)}, bf16[64,512]{1,0:T(8,128)(2,1)S(1)}, u32[]{:S(2)}, u32[]{:S(2)}) collective-permute-start(bf16[64,512]{1,0:T(8,128)(2,1)S(1)} %get-tuple-element.555), channel_id=1, source_target_pairs={{0,1},{1,2},{2,3},{3,4},{4,5},{5,6},{6,7},{7,8},{8,9},{9,10},{10,1... | collective-permute-start | bytes 196616 | tf_op jit(solution)/shard_map/while/body/eval_jaxpr/ppermute | solution.py:16
  132.6 3.6 %collective-permute-done.1 = bf16[64,512]{1,0:T(8,128)(2,1)S(1)} collective-permute-done((bf16[64,512]{1,0:T(8,128)(2,1)S(1)}, bf16[64,512]{1,0:T(8,128)(2,1)S(1)}, u32[]{:S(2)}, u32[]{:S(2)}) %collective-permute-start.1) | collective-permute-done | bytes 65568 | tf_op jit(solution)/shard_map/while/body/eval_jaxpr/ppermute | solution.py:16
  136.4 0.2 fusion.78
  136.7 0.4 fusion.76
  137.0 0.2 fusion.80
  137.4 0.2 fusion.82
  137.6 0.3 convolution_add_fusion.4
  138.0 0.9 copy.36
  (95 shorter events, 4.4 us)
Async XLA Ops:
  6.5 84.0 %copy-start = (bf16[1,128,2048]{2,1,0:T(8,128)(2,1)S(1)}, bf16[1,128,2048]{2,1,0:T(8,128)(2,1)}, u32[]{:S(2)}) copy-start(bf16[1,128,2048]{2,1,0:T(8,128)(2,1)} %param.6) | copy-start | bytes 1572868
  6.5 84.0 %all-gather.2.cloned.1.call-start = ((), (), s32[]{:S(2)}) async-start(), calls=%async_computation | async-start | bytes 9437184 | tf_op jit(solution)/shard_map/all_gather | solution.py:50
  96.2 9.8 %collective-permute-start = (bf16[128,512]{0,1:T(8,128)(2,1)S(1)}, bf16[128,512]{0,1:T(8,128)(2,1)S(1)}, u32[]{:S(2)}, u32[]{:S(2)}) collective-permute-start(bf16[128,512]{0,1:T(8,128)(2,1)S(1)} %get-tuple-element.556), channel_id=1, source_target_pairs={{1,0},{2,1},{3,2},{4,3},{5,4},{6,5},{7,6},{8,7},{9,8},{10,9},{11,1... | collective-permute-start | bytes 393224 | tf_op jit(solution)/shard_map/while/body/eval_jaxpr/ppermute | solution.py:16
  99.0 6.5 %collective-permute-start.1 = (bf16[64,512]{1,0:T(8,128)(2,1)S(1)}, bf16[64,512]{1,0:T(8,128)(2,1)S(1)}, u32[]{:S(2)}, u32[]{:S(2)}) collective-permute-start(bf16[64,512]{1,0:T(8,128)(2,1)S(1)} %get-tuple-element.555), channel_id=1, source_target_pairs={{0,1},{1,2},{2,3},{3,4},{4,5},{5,6},{6,7},{7,8},{8,9},{9,10},{10,1... | collective-permute-start | bytes 196616 | tf_op jit(solution)/shard_map/while/body/eval_jaxpr/ppermute | solution.py:16
  107.3 8.9 %collective-permute-start = (bf16[128,512]{0,1:T(8,128)(2,1)S(1)}, bf16[128,512]{0,1:T(8,128)(2,1)S(1)}, u32[]{:S(2)}, u32[]{:S(2)}) collective-permute-start(bf16[128,512]{0,1:T(8,128)(2,1)S(1)} %get-tuple-element.556), channel_id=1, source_target_pairs={{1,0},{2,1},{3,2},{4,3},{5,4},{6,5},{7,6},{8,7},{9,8},{10,9},{11,1... | collective-permute-start | bytes 393224 | tf_op jit(solution)/shard_map/while/body/eval_jaxpr/ppermute | solution.py:16
  109.2 6.5 %collective-permute-start.1 = (bf16[64,512]{1,0:T(8,128)(2,1)S(1)}, bf16[64,512]{1,0:T(8,128)(2,1)S(1)}, u32[]{:S(2)}, u32[]{:S(2)}) collective-permute-start(bf16[64,512]{1,0:T(8,128)(2,1)S(1)} %get-tuple-element.555), channel_id=1, source_target_pairs={{0,1},{1,2},{2,3},{3,4},{4,5},{5,6},{6,7},{7,8},{8,9},{9,10},{10,1... | collective-permute-start | bytes 196616 | tf_op jit(solution)/shard_map/while/body/eval_jaxpr/ppermute | solution.py:16
  117.5 8.9 %collective-permute-start = (bf16[128,512]{0,1:T(8,128)(2,1)S(1)}, bf16[128,512]{0,1:T(8,128)(2,1)S(1)}, u32[]{:S(2)}, u32[]{:S(2)}) collective-permute-start(bf16[128,512]{0,1:T(8,128)(2,1)S(1)} %get-tuple-element.556), channel_id=1, source_target_pairs={{1,0},{2,1},{3,2},{4,3},{5,4},{6,5},{7,6},{8,7},{9,8},{10,9},{11,1... | collective-permute-start | bytes 393224 | tf_op jit(solution)/shard_map/while/body/eval_jaxpr/ppermute | solution.py:16
  119.4 6.5 %collective-permute-start.1 = (bf16[64,512]{1,0:T(8,128)(2,1)S(1)}, bf16[64,512]{1,0:T(8,128)(2,1)S(1)}, u32[]{:S(2)}, u32[]{:S(2)}) collective-permute-start(bf16[64,512]{1,0:T(8,128)(2,1)S(1)} %get-tuple-element.555), channel_id=1, source_target_pairs={{0,1},{1,2},{2,3},{3,4},{4,5},{5,6},{6,7},{7,8},{8,9},{9,10},{10,1... | collective-permute-start | bytes 196616 | tf_op jit(solution)/shard_map/while/body/eval_jaxpr/ppermute | solution.py:16
  127.7 8.9 %collective-permute-start = (bf16[128,512]{0,1:T(8,128)(2,1)S(1)}, bf16[128,512]{0,1:T(8,128)(2,1)S(1)}, u32[]{:S(2)}, u32[]{:S(2)}) collective-permute-start(bf16[128,512]{0,1:T(8,128)(2,1)S(1)} %get-tuple-element.556), channel_id=1, source_target_pairs={{1,0},{2,1},{3,2},{4,3},{5,4},{6,5},{7,6},{8,7},{9,8},{10,9},{11,1... | collective-permute-start | bytes 393224 | tf_op jit(solution)/shard_map/while/body/eval_jaxpr/ppermute | solution.py:16
  129.7 6.5 %collective-permute-start.1 = (bf16[64,512]{1,0:T(8,128)(2,1)S(1)}, bf16[64,512]{1,0:T(8,128)(2,1)S(1)}, u32[]{:S(2)}, u32[]{:S(2)}) collective-permute-start(bf16[64,512]{1,0:T(8,128)(2,1)S(1)} %get-tuple-element.555), channel_id=1, source_target_pairs={{0,1},{1,2},{2,3},{3,4},{4,5},{5,6},{6,7},{7,8},{8,9},{9,10},{10,1... | collective-permute-start | bytes 196616 | tf_op jit(solution)/shard_map/while/body/eval_jaxpr/ppermute | solution.py:16
Sparse Core Ops, SparseCore 0:
  8.9 81.5 all-gather.1
where the time goes:
time: 146 us
  waiting for transfers between devices  93.8 us (64%)
  starting transfers between devices  17.7 us (12%)
  between operations  14.2 us (10%)
  matrix products  8.97 us (6%)
  other arithmetic  7.82 us (5%)
  local copies, waits for them, and re-layouts  2.63 us (2%)
    all_gather x1, waiting for transfers between devices, body(): lax.all_gather(qkv_weight, 'seq', axis=1, tiled=True)  78.3 us
    ppermute x8, starting transfers between devices, shifted(): lax.ppermute(value, axis, [(source, source + steps) for source in range(i...  17.7 us
    ppermute x8, waiting for transfers between devices, shifted(): lax.ppermute(value, axis, [(source, source + steps) for source in range(i...  14.8 us
    dot_general x1, matrix products, body(): jnp.dot(rows, lax.all_gather(qkv_weight, 'seq', axis=1, tiled=True), pref...  3.78 us
  transfers between devices with their start and end apart: 9, of which 5 were waited for; matrix products, arithmetic and copies ran while one was open for 5% of the time, Pallas kernels for 0%

commit v1 on v0

v1 whole, which is shorter than its diff:
```python
import functools
import math

import jax
import jax.numpy as jnp
import numpy as np
from jax import lax
from jax.experimental import pallas as pl
from jax.experimental.pallas import tpu as pltpu
from jax.sharding import PartitionSpec as P

QUERY_HEADS = 16
KEY_VALUE_HEADS = 4
HEAD_SIZE = 64
QUERY_PER_KV = 4
SPAN = 64
PAIR = 2 * HEAD_SIZE
QCOLS = QUERY_HEADS * HEAD_SIZE
KVCOLS = KEY_VALUE_HEADS * HEAD_SIZE
MESH = pl.DeviceIdType.MESH
SCALE = 0.125 * math.log2(math.e)


def kernel(
    parts, devices, steps, chunks, col_tile,
    tok_ref, w_ref, freq_ref, len_ref, order_ref, out_ref,
    tok_own, w_v, tok_in, back, full, pieces, kv, q_s, bias, cos_s, sin_s,
    local_sem, tok_send, tok_recv, back_send, back_recv, kv_send, kv_recv,
):
    me = lax.axis_index("seq")
    c = lax.axis_index("ctx")
    rows = tok_own.shape[0]
    cols = w_v.shape[1]
    tiles = cols // col_tile
    docs = len_ref.shape[1]
    direct = cols % 128 == 0
    per_chunk = rows // chunks

    def up_of(k):
        return jnp.where(c + k < devices, c + k, 2 * devices - 1 - c - k)

    w_copies = [
        pltpu.make_async_copy(
            w_ref.at[:, pl.ds(t * col_tile, col_tile)],
            w_v.at[:, pl.ds(t * col_tile, col_tile)],
            local_sem.at[1 + t],
        )
        for t in range(tiles)
    ]
    own_copy = pltpu.make_async_copy(tok_ref.at[0], tok_own, local_sem.at[0])

    barrier = pltpu.get_barrier_semaphore()
    for j in range(1, parts):
        pl.semaphore_signal(
            barrier, inc=1, device_id=(lax.rem(me + j, parts), c), device_id_type=MESH
        )
    expected = jnp.int32(parts - 1)
    for k in range(1, steps + 1):
        up = up_of(k)
        expected = expected + (up != c).astype(jnp.int32) + (c >= k).astype(jnp.int32)

        @pl.when(up != c)
        def _():
            pl.semaphore_signal(barrier, inc=1, device_id=(me, up), device_id_type=MESH)

        @pl.when(c >= k)
        def _():
            pl.semaphore_signal(barrier, inc=1, device_id=(me, c - k), device_id_type=MESH)

    own_copy.start()
    for t in reversed(range(tiles)):
        w_copies[t].start()
    pl.semaphore_wait(barrier, expected)

    def token_copy(j, h):
        part = pl.ds(h * per_chunk, per_chunk)
        return pltpu.make_async_remote_copy(
            src_ref=tok_ref.at[0, part],
            dst_ref=tok_in.at[j - 1, part],
            send_sem=tok_send.at[j - 1, h],
            recv_sem=tok_recv.at[j - 1, h],
            device_id=(lax.rem(me + j, parts), c),
            device_id_type=MESH,
        )

    def back_copy(j, h, t):
        part = pl.ds(h * per_chunk, per_chunk)
        lanes = pl.ds(t * col_tile, col_tile)
        if direct:
            start = pl.multiple_of(me * cols + t * col_tile, 128)
            target = full.at[part, pl.ds(start, col_tile)]
        else:
            target = pieces.at[me, part]
        return pltpu.make_async_remote_copy(
            src_ref=back.at[j - 1, part, lanes],
            dst_ref=target,
            send_sem=back_send.at[j - 1, h, t],
            recv_sem=back_recv.at[j - 1, h, t],
            device_id=(lax.rem(me + parts - j, parts), c),
            device_id_type=MESH,
        )

    for h in range(chunks):
        for j in range(1, parts):
            token_copy(j, h).start()

    row = lax.broadcasted_iota(jnp.int32, (SPAN, PAIR), 0)
    lane = lax.broadcasted_iota(jnp.int32, (SPAN, PAIR), 1)
    first_half = lax.rem(lane, HEAD_SIZE) < HEAD_SIZE // 2
    low = lane < HEAD_SIZE
    firsts = (c, 2 * devices - 1 - c)
    total_keys = (steps + 1) * SPAN
    for e in range(2):
        angle = (row + firsts[e] * SPAN).astype(jnp.float32) * freq_ref[...]
        cos_s[e] = jnp.cos(angle)
        sine = jnp.sin(angle)
        sin_s[e] = jnp.where(first_half, -sine, sine)
        key_at = lax.broadcasted_iota(jnp.int32, (SPAN, total_keys), 1)
        block = key_at // SPAN
        key_place = (firsts[e] - block) * SPAN + key_at - block * SPAN
        q_place = lax.broadcasted_iota(jnp.int32, (SPAN, total_keys), 0) + firsts[e] * SPAN
        doc_start = jnp.zeros((SPAN, total_keys), jnp.int32)
        end = jnp.int32(0)
        for d in range(docs):
            end = end + len_ref[0, d]
            doc_start = jnp.where(q_place >= end, end, doc_start)
        live = (key_place >= doc_start) & (key_place <= q_place)
        bias[e] = jnp.where(live, 0.0, -1e30)
    for k in range(1, steps + 1):

        @pl.when(c < k)
        def _():
            kv[0, k] = jnp.zeros((SPAN, 2 * KVCOLS), kv.dtype)

    def project(value, t):
        return jnp.dot(
            value, w_v[:, t * col_tile : (t + 1) * col_tile], preferred_element_type=jnp.float32
        ).astype(jnp.bfloat16)

    own_copy.wait()
    for t in reversed(range(tiles)):
        w_copies[t].wait()
        value = project(tok_own[...], t)
        if direct:
            start = pl.multiple_of(me * cols + t * col_tile, 128)
            full[:, pl.ds(start, col_tile)] = value
        else:
            pieces[me] = value

    for h in range(chunks):
        part = slice(h * per_chunk, (h + 1) * per_chunk)
        for j in range(1, parts):
            token_copy(j, h).wait_recv()
            for t in reversed(range(tiles)):
                back[j - 1, part, t * col_tile : (t + 1) * col_tile] = project(
                    tok_in[j - 1, part], t
                )
                back_copy(j, h, t).start()

    for t in reversed(range(tiles)):
        for h in range(chunks):
            for j in range(1, parts):
                back_copy(j, h, t).wait_recv()
    if not direct:
        for p in range(parts):
            full[:, p * cols : (p + 1) * cols] = pieces[p]

    flip = jnp.full((SPAN, PAIR), order_ref[0, 2 * c], jnp.int32) >= devices

    def pair_of(column):
        block = full[:, column : column + PAIR].astype(jnp.float32)
        one, two = block[:SPAN], block[SPAN:]
        return jnp.where(flip, two, one), jnp.where(flip, one, two)

    def turn(value, e):
        other = jnp.where(
            first_half, pltpu.roll(value, PAIR - HEAD_SIZE // 2, 1), pltpu.roll(value, HEAD_SIZE // 2, 1)
        )
        return value * cos_s[e] + other * sin_s[e]

    for b in range(KVCOLS // PAIR):
        both = pair_of(QCOLS + b * PAIR)
        values = pair_of(QCOLS + KVCOLS + b * PAIR)
        for e in range(2):
            kv[e, 0, :, b * PAIR : (b + 1) * PAIR] = turn(both[e], e).astype(jnp.bfloat16)
            kv[e, 0, :, KVCOLS + b * PAIR : KVCOLS + (b + 1) * PAIR] = values[e].astype(jnp.bfloat16)

    def early_copy(k):
        wrapped = (c + k >= devices).astype(jnp.int32)
        return pltpu.make_async_remote_copy(
            src_ref=kv.at[0, 0],
            dst_ref=kv.at[wrapped, k],
            send_sem=kv_send.at[0, k - 1],
            recv_sem=kv_recv.at[wrapped, k - 1],
            device_id=(me, up_of(k)),
            device_id_type=MESH,
        )

    def late_copy(k):
        return pltpu.make_async_remote_copy(
            src_ref=kv.at[1, 0],
            dst_ref=kv.at[1, k],
            send_sem=kv_send.at[1, k - 1],
            recv_sem=kv_recv.at[1, k - 1],
            device_id=(me, jnp.maximum(c - k, 0)),
            device_id_type=MESH,
        )

    def arrival(e, k):
        return pltpu.make_async_remote_copy(
            src_ref=kv.at[e, 0],
            dst_ref=kv.at[e, k],
            send_sem=kv_send.at[e, k - 1],
            recv_sem=kv_recv.at[e, k - 1],
            device_id=(me, up_of(k)),
            device_id_type=MESH,
        )

    for k in reversed(range(1, steps + 1)):

        @pl.when(up_of(k) != c)
        def _():
            early_copy(k).start()

        @pl.when(c >= k)
        def _():
            late_copy(k).start()

        @pl.when(up_of(k) == c)
        def _():
            kv[1, k] = kv[0, 0]

    for b in range(QCOLS // PAIR):
        both = pair_of(b * PAIR)
        g = 2 * b // QUERY_PER_KV
        for e in range(2):
            turned = turn(both[e], e)
            swapped = pltpu.roll(turned, HEAD_SIZE, 1)
            for s in range(2):
                i = (2 * b + s) % QUERY_PER_KV
                placed = turned if s == g % 2 else swapped
                keep = low if g % 2 == 0 else ~low
                q_s[e, g, i * SPAN : (i + 1) * SPAN] = jnp.where(keep, placed, 0.0).astype(
                    jnp.bfloat16
                )

    for k in range(1, steps + 1):

        @pl.when(c >= k)
        def _():
            arrival(0, k).wait_recv()

        @pl.when(up_of(k) != c)
        def _():
            arrival(1, k).wait_recv()

    for g in range(KEY_VALUE_HEADS):
        pair = (g // 2) * PAIR
        outs = []
        for e in range(2):
            keys = kv[e, :, :, pair : pair + PAIR].reshape(total_keys, PAIR)
            values = kv[e, :, :, KVCOLS + pair : KVCOLS + pair + PAIR].reshape(total_keys, PAIR)
            scores = lax.dot_general(
                q_s[e, g], keys, (((1,), (1,)), ((), ())), preferred_element_type=jnp.float32
            )
            scores = scores.reshape(QUERY_PER_KV, SPAN, total_keys) * SCALE + bias[e][None]
            scores = scores.reshape(QUERY_PER_KV * SPAN, total_keys)
            top = jnp.max(scores, axis=1, keepdims=True)
            weights = jnp.exp2(scores - top)
            total = jnp.sum(weights, axis=1, keepdims=True)
            summed = jnp.dot(
                weights.astype(jnp.bfloat16), values, preferred_element_type=jnp.float32
            )
            outs.append(summed / total)
        for m in range(QUERY_PER_KV // 2):
            made = []
            for e in range(2):
                one = outs[e][(2 * m) * SPAN : (2 * m + 1) * SPAN]
                two = outs[e][(2 * m + 1) * SPAN : (2 * m + 2) * SPAN]
                if g % 2 == 0:
                    two = pltpu.roll(two, HEAD_SIZE, 1)
                else:
                    one = pltpu.roll(one, HEAD_SIZE, 1)
                made.append(jnp.where(low, one, two))
            at = (g * QUERY_PER_KV + 2 * m) * HEAD_SIZE
            out_ref[0, :SPAN, at : at + PAIR] = jnp.where(flip, made[1], made[0]).astype(jnp.bfloat16)
            out_ref[0, SPAN:, at : at + PAIR] = jnp.where(flip, made[0], made[1]).astype(jnp.bfloat16)

    for j in range(1, parts):
        for h in range(chunks):
            token_copy(j, h).wait_send()
            for t in range(tiles):
                back_copy(j, h, t).wait_send()
    for k in range(1, steps + 1):

        @pl.when(up_of(k) != c)
        def _():
            early_copy(k).wait_send()

        @pl.when(c >= k)
        def _():
            late_copy(k).wait_send()


def body(parts, devices, tokens, qkv_weight, doc_lengths, span_order):
    _, rows, width = tokens.shape
    cols = qkv_weight.shape[1]
    steps = devices // 4
    chunks = 2
    col_tile = 256 if cols % 256 == 0 else cols
    tiles = cols // col_tile
    half = HEAD_SIZE // 2
    freq = 500000.0 ** (-np.arange(half, dtype=np.float64) * 2.0 / HEAD_SIZE)
    freq = np.tile(freq.astype(np.float32), PAIR // half)[None]
    pieces_shape = (parts, rows, cols) if cols % 128 else (1, 16, 128)
    return pl.pallas_call(
        functools.partial(kernel, parts, devices, steps, chunks, col_tile),
        out_shape=jax.ShapeDtypeStruct((1, rows, QCOLS), jnp.bfloat16),
        in_specs=[
            pl.BlockSpec(memory_space=pl.ANY),
            pl.BlockSpec(memory_space=pl.ANY),
            pl.BlockSpec(memory_space=pltpu.VMEM),
            pl.BlockSpec(memory_space=pltpu.SMEM),
            pl.BlockSpec(memory_space=pltpu.SMEM),
        ],
        out_specs=pl.BlockSpec(memory_space=pltpu.VMEM),
        scratch_shapes=[
            pltpu.VMEM((rows, width), jnp.bfloat16),
            pltpu.VMEM((width, cols), jnp.bfloat16),
            pltpu.VMEM((parts - 1, rows, width), jnp.bfloat16),
            pltpu.VMEM((parts - 1, rows, cols), jnp.bfloat16),
            pltpu.VMEM((rows, parts * cols), jnp.bfloat16),
            pltpu.VMEM(pieces_shape, jnp.bfloat16),
            pltpu.VMEM((2, steps + 1, SPAN, 2 * KVCOLS), jnp.bfloat16),
            pltpu.VMEM((2, KEY_VALUE_HEADS, QUERY_PER_KV * SPAN, PAIR), jnp.bfloat16),
            pltpu.VMEM((2, SPAN, (steps + 1) * SPAN), jnp.float32),
            pltpu.VMEM((2, SPAN, PAIR), jnp.float32),
            pltpu.VMEM((2, SPAN, PAIR), jnp.float32),
            pltpu.SemaphoreType.DMA((1 + tiles,)),
            pltpu.SemaphoreType.DMA((parts - 1, chunks)),
            pltpu.SemaphoreType.DMA((parts - 1, chunks)),
            pltpu.SemaphoreType.DMA((parts - 1, chunks, tiles)),
            pltpu.SemaphoreType.DMA((parts - 1, chunks, tiles)),
            pltpu.SemaphoreType.DMA((2, steps)),
            pltpu.SemaphoreType.DMA((2, steps)),
        ],
        compiler_params=pltpu.CompilerParams(
            collective_id=0, has_side_effects=True, vmem_limit_bytes=48 * 1024 * 1024
        ),
    )(tokens, qkv_weight, jnp.asarray(freq), doc_lengths, span_order)


def solution(mesh):
    placed = (P("seq", "ctx", None), P(None, "seq"), P("seq", None), P("seq", None))
    return jax.shard_map(
        functools.partial(body, mesh.shape["seq"], mesh.shape["ctx"]),
        mesh=mesh,
        in_specs=placed,
        out_specs=P("seq", "ctx", None),
        check_vma=False,
    )
```

time: 146 us -> 37 us (0.25)
  the two profiles are of different devices: /device:TPU:8 before, /device:TPU:25 now
where the time goes in v1:
time: 37 us; the launch traced here: 36.7 us
  Pallas kernels  31.1 us (84%)
  local copies, waits for them, and re-layouts  5.6 us (15%)
    pallas_call x1, Pallas kernels, body(): pl.pallas_call(functools.partial(kernel, parts, devices, steps, chunks, c...  31.1 us
    unnamed x11, local copies, waits for them, and re-layouts  5.6 us

profile of v1, /device:TPU:25, one launch (start us, length us, event | category | flops | bytes accessed | tf_op | source)
XLA Modules:
  0.0 36.7 jit_solution(17546116402287871769)
XLA Ops:
  0.0 0.0 copy-start
  0.0 1.9 %copy-done = bf16[2048,768]{1,0:T(8,128)(2,1)S(1)} copy-done((bf16[2048,768]{1,0:T(8,128)(2,1)S(1)}, bf16[2048,768]{1,0:T(8,128)(2,1)}, u32[]{:S(2)}) %copy-start) | copy-done | bytes 3145752
  1.9 0.0 copy-start.1
  1.9 1.0 %copy-done.1 = bf16[1,128,2048]{2,1,0:T(8,128)(2,1)S(1)} copy-done((bf16[1,128,2048]{2,1,0:T(8,128)(2,1)S(1)}, bf16[1,128,2048]{2,1,0:T(8,128)(2,1)}, u32[]{:S(2)}) %copy-start.1) | copy-done | bytes 524312
  2.9 0.0 copy-start.2
  2.9 0.7 %copy-done.2 = s32[1,12]{1,0:T(1,128)S(1)} copy-done((s32[1,12]{1,0:T(1,128)S(1)}, s32[1,12]{1,0:T(1,128)}, u32[]{:S(2)}) %copy-start.2) | copy-done | bytes 72
  3.6 0.0 copy-start.3
  3.6 0.7 %copy-done.3 = s32[1,32]{1,0:T(1,128)S(1)} copy-done((s32[1,32]{1,0:T(1,128)S(1)}, s32[1,32]{1,0:T(1,128)}, u32[]{:S(2)}) %copy-start.3) | copy-done | bytes 152
  4.2 0.0 copy-start.4
  4.2 0.7 %copy-done.4 = f32[1,128]{1,0:T(1,128)S(1)} copy-done((f32[1,128]{1,0:T(1,128)S(1)}, f32[1,128]{1,0:T(1,128)}, u32[]{:S(2)}) %copy-start.4) | copy-done | bytes 536
  4.9 31.1 %shard_map.55 = bf16[1,128,1024]{2,1,0:T(8,128)(2,1)S(1)} custom-call(bf16[1,128,2048]{2,1,0:T(8,128)(2,1)S(1)} %copy-done.1, bf16[2048,768]{1,0:T(8,128)(2,1)S(1)} %copy-done, f32[1,128]{1,0:T(1,128)S(1)} %copy-done.4, s32[1,12]{1,0:T(1,128)S(1)} %copy-done.2, s32[1,32]{1,0:T(1,128)S(1)} %copy-done.3), custom_call_target="tpu_custom_call" | custom-call | tf_op jit(solution)/shard_map/pallas_call | solution.py:316
  36.0 0.7 %copy.7 = bf16[1,128,1024]{2,1,0:T(8,128)(2,1)} copy(bf16[1,128,1024]{2,1,0:T(8,128)(2,1)S(1)} %shard_map.55) | data formatting | bytes 524288
Async XLA Ops:
  0.0 1.9 %copy-start = (bf16[2048,768]{1,0:T(8,128)(2,1)S(1)}, bf16[2048,768]{1,0:T(8,128)(2,1)}, u32[]{:S(2)}) copy-start(bf16[2048,768]{1,0:T(8,128)(2,1)} %w_ref.1) | copy-start | bytes 9437188
  1.9 1.0 %copy-start.1 = (bf16[1,128,2048]{2,1,0:T(8,128)(2,1)S(1)}, bf16[1,128,2048]{2,1,0:T(8,128)(2,1)}, u32[]{:S(2)}) copy-start(bf16[1,128,2048]{2,1,0:T(8,128)(2,1)} %tok_ref.1) | copy-start | bytes 1572868
  2.9 0.7 %copy-start.2 = (s32[1,12]{1,0:T(1,128)S(1)}, s32[1,12]{1,0:T(1,128)}, u32[]{:S(2)}) copy-start(s32[1,12]{1,0:T(1,128)} %len_ref.1) | copy-start | bytes 148
  3.6 0.7 %copy-start.3 = (s32[1,32]{1,0:T(1,128)S(1)}, s32[1,32]{1,0:T(1,128)}, u32[]{:S(2)}) copy-start(s32[1,32]{1,0:T(1,128)} %order_ref.1) | copy-start | bytes 388
  4.2 0.7 %copy-start.4 = (f32[1,128]{1,0:T(1,128)S(1)}, f32[1,128]{1,0:T(1,128)}, u32[]{:S(2)}) copy-start(f32[1,128]{1,0:T(1,128)} %constant.2.clone.freq_ref) | copy-start | bytes 1540

commit v2 on v1

--- a/solution.py
+++ b/solution.py
@@ -22,9 +22,9 @@
 
 
 def kernel(
-    parts, devices, steps, chunks, col_tile,
+    parts, devices, steps, chunks, ahead, col_tile,
     tok_ref, w_ref, freq_ref, len_ref, order_ref, out_ref,
-    tok_own, w_v, tok_in, back, full, pieces, kv, q_s, bias, cos_s, sin_s,
+    tok_raw, tok_own, w_v, tok_in, back, full, pieces, kv, q_s, bias, cos_s, sin_s, out_s,
     local_sem, tok_send, tok_recv, back_send, back_recv, kv_send, kv_recv,
 ):
     me = lax.axis_index("seq")
@@ -35,9 +35,17 @@
     docs = len_ref.shape[1]
     direct = cols % 128 == 0
     per_chunk = rows // chunks
+    per_span = chunks // 2
 
     def up_of(k):
         return jnp.where(c + k < devices, c + k, 2 * devices - 1 - c - k)
+
+    order_mine = order_ref[0, 2 * c]
+
+    def choose(one, two):
+        swap = jnp.full(one.shape, order_mine, jnp.int32) >= devices
+        one, two = one.astype(jnp.float32), two.astype(jnp.float32)
+        return jnp.where(swap, two, one).astype(jnp.bfloat16)
 
     w_copies = [
         pltpu.make_async_copy(
@@ -47,7 +55,8 @@
         )
         for t in range(tiles)
     ]
-    own_copy = pltpu.make_async_copy(tok_ref.at[0], tok_own, local_sem.at[0])
+    raw_copy = pltpu.make_async_copy(tok_ref.at[0], tok_raw, local_sem.at[0])
+    raw_copy.start()
 
     barrier = pltpu.get_barrier_semaphore()
     for j in range(1, parts):
@@ -67,15 +76,17 @@
         def _():
             pl.semaphore_signal(barrier, inc=1, device_id=(me, c - k), device_id_type=MESH)
 
-    own_copy.start()
+    raw_copy.wait()
     for t in reversed(range(tiles)):
         w_copies[t].start()
+    tok_own[:SPAN] = choose(tok_raw[:SPAN], tok_raw[SPAN:])
+    tok_own[SPAN:] = choose(tok_raw[SPAN:], tok_raw[:SPAN])
     pl.semaphore_wait(barrier, expected)
 
     def token_copy(j, h):
         part = pl.ds(h * per_chunk, per_chunk)
         return pltpu.make_async_remote_copy(
-            src_ref=tok_ref.at[0, part],
+            src_ref=tok_own.at[part],
             dst_ref=tok_in.at[j - 1, part],
             send_sem=tok_send.at[j - 1, h],
             recv_sem=tok_recv.at[j - 1, h],
@@ -100,16 +111,22 @@
             device_id_type=MESH,
         )
 
-    for h in range(chunks):
+    def send_tokens(h):
         for j in range(1, parts):
             token_copy(j, h).start()
 
+    for h in range(min(ahead, chunks)):
+        send_tokens(h)
+
     row = lax.broadcasted_iota(jnp.int32, (SPAN, PAIR), 0)
-    lane = lax.broadcasted_iota(jnp.int32, (SPAN, PAIR), 1)
-    first_half = lax.rem(lane, HEAD_SIZE) < HEAD_SIZE // 2
-    low = lane < HEAD_SIZE
     firsts = (c, 2 * devices - 1 - c)
     total_keys = (steps + 1) * SPAN
+
+    def half_masks(count):
+        lane = lax.broadcasted_iota(jnp.int32, (count, PAIR), 1)
+        return lax.rem(lane, HEAD_SIZE) < HEAD_SIZE // 2, lane < HEAD_SIZE
+
+    first_half, low = half_masks(SPAN)
     for e in range(2):
         angle = (row + firsts[e] * SPAN).astype(jnp.float32) * freq_ref[...]
         cos_s[e] = jnp.cos(angle)
@@ -137,7 +154,6 @@
             value, w_v[:, t * col_tile : (t + 1) * col_tile], preferred_element_type=jnp.float32
         ).astype(jnp.bfloat16)
 
-    own_copy.wait()
     for t in reversed(range(tiles)):
         w_copies[t].wait()
         value = project(tok_own[...], t)
@@ -147,7 +163,7 @@
         else:
             pieces[me] = value
 
-    for h in range(chunks):
+    def serve(h):
         part = slice(h * per_chunk, (h + 1) * per_chunk)
         for j in range(1, parts):
             token_copy(j, h).wait_recv()
@@ -157,85 +173,96 @@
                 )
                 back_copy(j, h, t).start()
 
-    for t in reversed(range(tiles)):
-        for h in range(chunks):
+    def arrived_back(h, which):
+        for t in which:
             for j in range(1, parts):
                 back_copy(j, h, t).wait_recv()
-    if not direct:
-        for p in range(parts):
-            full[:, p * cols : (p + 1) * cols] = pieces[p]
-
-    flip = jnp.full((SPAN, PAIR), order_ref[0, 2 * c], jnp.int32) >= devices
-
-    def pair_of(column):
-        block = full[:, column : column + PAIR].astype(jnp.float32)
-        one, two = block[:SPAN], block[SPAN:]
-        return jnp.where(flip, two, one), jnp.where(flip, one, two)
-
-    def turn(value, e):
+
+    kv_tiles = [
+        t
+        for t in range(tiles)
+        if any(p * cols + (t + 1) * col_tile > QCOLS for p in range(parts))
+    ]
+    q_tiles = [t for t in range(tiles) if t not in kv_tiles]
+
+    def turn(value, e, at):
+        count = value.shape[0]
         other = jnp.where(
-            first_half, pltpu.roll(value, PAIR - HEAD_SIZE // 2, 1), pltpu.roll(value, HEAD_SIZE // 2, 1)
-        )
-        return value * cos_s[e] + other * sin_s[e]
-
-    for b in range(KVCOLS // PAIR):
-        both = pair_of(QCOLS + b * PAIR)
-        values = pair_of(QCOLS + KVCOLS + b * PAIR)
-        for e in range(2):
-            kv[e, 0, :, b * PAIR : (b + 1) * PAIR] = turn(both[e], e).astype(jnp.bfloat16)
-            kv[e, 0, :, KVCOLS + b * PAIR : KVCOLS + (b + 1) * PAIR] = values[e].astype(jnp.bfloat16)
-
-    def early_copy(k):
+            half_masks(count)[0],
+            pltpu.roll(value, PAIR - HEAD_SIZE // 2, 1),
+            pltpu.roll(value, HEAD_SIZE // 2, 1),
+        )
+        return value * cos_s[e, at : at + count] + other * sin_s[e, at : at + count]
+
+    def early_copy(k, i):
         wrapped = (c + k >= devices).astype(jnp.int32)
+        part = pl.ds(i * per_chunk, per_chunk)
         return pltpu.make_async_remote_copy(
-            src_ref=kv.at[0, 0],
-            dst_ref=kv.at[wrapped, k],
-            send_sem=kv_send.at[0, k - 1],
-            recv_sem=kv_recv.at[wrapped, k - 1],
+            src_ref=kv.at[0, 0, part],
+            dst_ref=kv.at[wrapped, k, part],
+            send_sem=kv_send.at[0, k - 1, i],
+            recv_sem=kv_recv.at[wrapped, k - 1, i],
             device_id=(me, up_of(k)),
             device_id_type=MESH,
         )
 
-    def late_copy(k):
+    def late_copy(k, i):
+        part = pl.ds(i * per_chunk, per_chunk)
         return pltpu.make_async_remote_copy(
-            src_ref=kv.at[1, 0],
-            dst_ref=kv.at[1, k],
-            send_sem=kv_send.at[1, k - 1],
-            recv_sem=kv_recv.at[1, k - 1],
+            src_ref=kv.at[1, 0, part],
+            dst_ref=kv.at[1, k, part],
+            send_sem=kv_send.at[1, k - 1, i],
+            recv_sem=kv_recv.at[1, k - 1, i],
             device_id=(me, jnp.maximum(c - k, 0)),
             device_id_type=MESH,
         )
 
-    def arrival(e, k):
+    def arrival(e, k, i):
+        part = pl.ds(i * per_chunk, per_chunk)
         return pltpu.make_async_remote_copy(
-            src_ref=kv.at[e, 0],
-            dst_ref=kv.at[e, k],
-            send_sem=kv_send.at[e, k - 1],
-            recv_sem=kv_recv.at[e, k - 1],
+            src_ref=kv.at[e, 0, part],
+            dst_ref=kv.at[e, k, part],
+            send_sem=kv_send.at[e, k - 1, i],
+            recv_sem=kv_recv.at[e, k - 1, i],
             device_id=(me, up_of(k)),
             device_id_type=MESH,
         )
 
-    for k in reversed(range(1, steps + 1)):
-
-        @pl.when(up_of(k) != c)
-        def _():
-            early_copy(k).start()
-
-        @pl.when(c >= k)
-        def _():
-            late_copy(k).start()
-
-        @pl.when(up_of(k) == c)
-        def _():
-            kv[1, k] = kv[0, 0]
-
-    for b in range(QCOLS // PAIR):
-        both = pair_of(b * PAIR)
-        g = 2 * b // QUERY_PER_KV
-        for e in range(2):
-            turned = turn(both[e], e)
+    def spread(h):
+        e, i = h // per_span, h % per_span
+        at = i * per_chunk
+        part = slice(h * per_chunk, (h + 1) * per_chunk)
+        arrived_back(h, kv_tiles)
+        if not direct:
+            for p in range(parts):
+                full[part, p * cols : (p + 1) * cols] = pieces[p, part]
+        for b in range(KVCOLS // PAIR):
+            block = full[part, QCOLS + b * PAIR : QCOLS + (b + 1) * PAIR].astype(jnp.float32)
+            kv[e, 0, at : at + per_chunk, b * PAIR : (b + 1) * PAIR] = turn(block, e, at).astype(
+                jnp.bfloat16
+            )
+        kv[e, 0, at : at + per_chunk, KVCOLS:] = full[part, QCOLS + KVCOLS :]
+        for k in reversed(range(1, steps + 1)):
+            if e == 0:
+
+                @pl.when(up_of(k) != c)
+                def _():
+                    early_copy(k, i).start()
+
+            else:
+
+                @pl.when(c >= k)
+                def _():
+                    late_copy(k, i).start()
+
+    def queries(e):
+        for i in range(per_span):
+            arrived_back(e * per_span + i, q_tiles)
+        for b in range(QCOLS // PAIR):
+            block = full[e * SPAN : (e + 1) * SPAN, b * PAIR : (b + 1) * PAIR]
+            turned = turn(block.astype(jnp.float32), e, 0)
             swapped = pltpu.roll(turned, HEAD_SIZE, 1)
+            g = 2 * b // QUERY_PER_KV
             for s in range(2):
                 i = (2 * b + s) % QUERY_PER_KV
                 placed = turned if s == g % 2 else swapped
@@ -244,20 +271,9 @@
                     jnp.bfloat16
                 )
 
-    for k in range(1, steps + 1):
-
-        @pl.when(c >= k)
-        def _():
-            arrival(0, k).wait_recv()
-
-        @pl.when(up_of(k) != c)
-        def _():
-            arrival(1, k).wait_recv()
-
-    for g in range(KEY_VALUE_HEADS):
-        pair = (g // 2) * PAIR
-        outs = []
-        for e in range(2):
+    def attend(e):
+        for g in range(KEY_VALUE_HEADS):
+            pair = (g // 2) * PAIR
             keys = kv[e, :, :, pair : pair + PAIR].reshape(total_keys, PAIR)
             values = kv[e, :, :, KVCOLS + pair : KVCOLS + pair + PAIR].reshape(total_keys, PAIR)
             scores = lax.dot_general(
@@ -271,20 +287,54 @@
             summed = jnp.dot(
                 weights.astype(jnp.bfloat16), values, preferred_element_type=jnp.float32
             )
-            outs.append(summed / total)
-        for m in range(QUERY_PER_KV // 2):
-            made = []
-            for e in range(2):
-                one = outs[e][(2 * m) * SPAN : (2 * m + 1) * SPAN]
-                two = outs[e][(2 * m + 1) * SPAN : (2 * m + 2) * SPAN]
+            outs = summed / total
+            for m in range(QUERY_PER_KV // 2):
+                one = outs[(2 * m) * SPAN : (2 * m + 1) * SPAN]
+                two = outs[(2 * m + 1) * SPAN : (2 * m + 2) * SPAN]
                 if g % 2 == 0:
                     two = pltpu.roll(two, HEAD_SIZE, 1)
                 else:
                     one = pltpu.roll(one, HEAD_SIZE, 1)
-                made.append(jnp.where(low, one, two))
-            at = (g * QUERY_PER_KV + 2 * m) * HEAD_SIZE
-            out_ref[0, :SPAN, at : at + PAIR] = jnp.where(flip, made[1], made[0]).astype(jnp.bfloat16)
-            out_ref[0, SPAN:, at : at + PAIR] = jnp.where(flip, made[0], made[1]).astype(jnp.bfloat16)
+                at = (g * QUERY_PER_KV + 2 * m) * HEAD_SIZE
+                out_s[e * SPAN : (e + 1) * SPAN, at : at + PAIR] = jnp.where(low, one, two).astype(
+                    jnp.bfloat16
+                )
+
+    for h in range(chunks):
+        serve(h)
+        if h + ahead < chunks:
+            send_tokens(h + ahead)
+        if h >= 1:
+            spread(h - 1)
+        if h == chunks - 1:
+            queries(0)
+    spread(chunks - 1)
+
+    for k in range(1, steps + 1):
+
+        @pl.when(up_of(k) == c)
+        def _():
+            kv[1, k] = kv[0, 0]
+
+    for k in range(1, steps + 1):
+
+        @pl.when(c >= k)
+        def _():
+            for i in range(per_span):
+                arrival(0, k, i).wait_recv()
+
+    attend(0)
+    queries(1)
+    for k in range(1, steps + 1):
+
+        @pl.when(up_of(k) != c)
+        def _():
+            for i in range(per_span):
+                arrival(1, k, i).wait_recv()
+
+    attend(1)
+    out_ref[0, :SPAN] = choose(out_s[:SPAN], out_s[SPAN:])
+    out_ref[0, SPAN:] = choose(out_s[SPAN:], out_s[:SPAN])
 
     for j in range(1, parts):
         for h in range(chunks):
@@ -295,18 +345,21 @@
 
         @pl.when(up_of(k) != c)
         def _():
-            early_copy(k).wait_send()
+            for i in range(per_span):
+                early_copy(k, i).wait_send()
 
         @pl.when(c >= k)
         def _():
-            late_copy(k).wait_send()
+            for i in range(per_span):
+                late_copy(k, i).wait_send()
 
 
 def body(parts, devices, tokens, qkv_weight, doc_lengths, span_order):
     _, rows, width = tokens.shape
     cols = qkv_weight.shape[1]
     steps = devices // 4
-    chunks = 2
+    chunks = 4
+    ahead = 3
     col_tile = 256 if cols % 256 == 0 else cols
     tiles = cols // col_tile
     half = HEAD_SIZE // 2
@@ -314,7 +367,7 @@
     freq = np.tile(freq.astype(np.float32), PAIR // half)[None]
     pieces_shape = (parts, rows, cols) if cols % 128 else (1, 16, 128)
     return pl.pallas_call(
-        functools.partial(kernel, parts, devices, steps, chunks, col_tile),
+        functools.partial(kernel, parts, devices, steps, chunks, ahead, col_tile),
         out_shape=jax.ShapeDtypeStruct((1, rows, QCOLS), jnp.bfloat16),
         in_specs=[
             pl.BlockSpec(memory_space=pl.ANY),
@@ -326,6 +379,7 @@
         out_specs=pl.BlockSpec(memory_space=pltpu.VMEM),
         scratch_shapes=[
             pltpu.VMEM((rows, width), jnp.bfloat16),
+            pltpu.VMEM((rows, width), jnp.bfloat16),
             pltpu.VMEM((width, cols), jnp.bfloat16),
             pltpu.VMEM((parts - 1, rows, width), jnp.bfloat16),
             pltpu.VMEM((parts - 1, rows, cols), jnp.bfloat16),
@@ -336,16 +390,17 @@
             pltpu.VMEM((2, SPAN, (steps + 1) * SPAN), jnp.float32),
             pltpu.VMEM((2, SPAN, PAIR), jnp.float32),
             pltpu.VMEM((2, SPAN, PAIR), jnp.float32),
+            pltpu.VMEM((rows, QCOLS), jnp.bfloat16),
             pltpu.SemaphoreType.DMA((1 + tiles,)),
             pltpu.SemaphoreType.DMA((parts - 1, chunks)),
             pltpu.SemaphoreType.DMA((parts - 1, chunks)),
             pltpu.SemaphoreType.DMA((parts - 1, chunks, tiles)),
             pltpu.SemaphoreType.DMA((parts - 1, chunks, tiles)),
-            pltpu.SemaphoreType.DMA((2, steps)),
-            pltpu.SemaphoreType.DMA((2, steps)),
+            pltpu.SemaphoreType.DMA((2, steps, chunks // 2)),
+            pltpu.SemaphoreType.DMA((2, steps, chunks // 2)),
         ],
         compiler_params=pltpu.CompilerParams(
-            collective_id=0, has_side_effects=True, vmem_limit_bytes=48 * 1024 * 1024
+            collective_id=0, has_side_effects=True, vmem_limit_bytes=62 * 1024 * 1024
         ),
     )(tokens, qkv_weight, jnp.asarray(freq), doc_lengths, span_order)
 

time: 37 us -> 31.3 us (0.85)
  the two profiles are of different devices: /device:TPU:25 before, /device:TPU:0 now
where the time goes in v2:
time: 31.3 us; the launch traced here: 31.1 us
  Pallas kernels  29.4 us (94%)
  local copies, waits for them, and re-layouts  1.67 us (5%)
    pallas_call x1, Pallas kernels, body(): pl.pallas_call(functools.partial(kernel, parts, devices, steps, chunks, a...  29.4 us
    unnamed x1, local copies, waits for them, and re-layouts  1.67 us

profile of v2, /device:TPU:0, one launch (start us, length us, event | category | flops | bytes accessed | tf_op | source)
XLA Modules:
  0.0 31.1 jit_solution(12443389070932564917)
XLA Ops:
  0.0 29.4 %shard_map.55 = bf16[1,128,1024]{2,1,0:T(8,128)(2,1)} custom-call(bf16[1,128,2048]{2,1,0:T(8,128)(2,1)} %tok_ref.1, bf16[2048,768]{1,0:T(8,128)(2,1)} %w_ref.1, f32[1,128]{1,0:T(1,128)} %constant.2.clone.freq_ref, s32[1,12]{1,0:T(1,128)} %len_ref.1, s32[1,32]{1,0:T(1,128)} %order_ref.1), custom_call_target="tpu_custom_call" | custom-call | tf_op jit(solution)/shard_map/pallas_call | solution.py:369
  29.4 1.7 %copy.7 = bf16[1,128,1024]{2,1,0:T(8,128)(2,1)} copy(bf16[1,128,1024]{2,1,0:T(8,128)(2,1)} %shard_map.55) | data formatting | bytes 524288

commit v3 on v2

--- a/solution.py
+++ b/solution.py
@@ -23,7 +23,7 @@
 
 def kernel(
     parts, devices, steps, chunks, ahead, col_tile,
-    tok_ref, w_ref, freq_ref, len_ref, order_ref, out_ref,
+    tok_ref, w_ref, len_ref, order_ref, out_ref,
     tok_raw, tok_own, w_v, tok_in, back, full, pieces, kv, q_s, bias, cos_s, sin_s, out_s,
     local_sem, tok_send, tok_recv, back_send, back_recv, kv_send, kv_recv,
 ):
@@ -115,8 +115,16 @@
         for j in range(1, parts):
             token_copy(j, h).start()
 
+    split = direct and (parts - 1) * cols <= QCOLS
+    last = me == parts - 1
     for h in range(min(ahead, chunks)):
         send_tokens(h)
+    if split:
+
+        @pl.when(jnp.logical_not(last))
+        def _():
+            for h in range(ahead, chunks):
+                send_tokens(h)
 
     row = lax.broadcasted_iota(jnp.int32, (SPAN, PAIR), 0)
     firsts = (c, 2 * devices - 1 - c)
@@ -127,8 +135,12 @@
         return lax.rem(lane, HEAD_SIZE) < HEAD_SIZE // 2, lane < HEAD_SIZE
 
     first_half, low = half_masks(SPAN)
+    index = lax.rem(lax.broadcasted_iota(jnp.int32, (1, PAIR), 1), HEAD_SIZE // 2)
+    freq = jnp.zeros((1, PAIR), jnp.float32)
+    for i in range(HEAD_SIZE // 2):
+        freq = jnp.where(index == i, np.float32(500000.0 ** (-2.0 * i / HEAD_SIZE)), freq)
     for e in range(2):
-        angle = (row + firsts[e] * SPAN).astype(jnp.float32) * freq_ref[...]
+        angle = (row + firsts[e] * SPAN).astype(jnp.float32) * freq
         cos_s[e] = jnp.cos(angle)
         sine = jnp.sin(angle)
         sin_s[e] = jnp.where(first_half, -sine, sine)
@@ -228,11 +240,11 @@
             device_id_type=MESH,
         )
 
-    def spread(h):
+    def spread(h, which):
         e, i = h // per_span, h % per_span
         at = i * per_chunk
         part = slice(h * per_chunk, (h + 1) * per_chunk)
-        arrived_back(h, kv_tiles)
+        arrived_back(h, which)
         if not direct:
             for p in range(parts):
                 full[part, p * cols : (p + 1) * cols] = pieces[p, part]
@@ -256,8 +268,15 @@
                     late_copy(k, i).start()
 
     def queries(e):
-        for i in range(per_span):
-            arrived_back(e * per_span + i, q_tiles)
+        def rest(which):
+            for i in range(per_span):
+                arrived_back(e * per_span + i, which)
+
+        if split:
+            pl.when(last)(lambda: rest(range(tiles)))
+            pl.when(jnp.logical_not(last))(lambda: rest(q_tiles))
+        else:
+            rest(q_tiles)
         for b in range(QCOLS // PAIR):
             block = full[e * SPAN : (e + 1) * SPAN, b * PAIR : (b + 1) * PAIR]
             turned = turn(block.astype(jnp.float32), e, 0)
@@ -300,15 +319,35 @@
                     jnp.bfloat16
                 )
 
-    for h in range(chunks):
-        serve(h)
-        if h + ahead < chunks:
-            send_tokens(h + ahead)
-        if h >= 1:
-            spread(h - 1)
-        if h == chunks - 1:
-            queries(0)
-    spread(chunks - 1)
+    if split:
+
+        @pl.when(last)
+        def _():
+            for h in range(chunks):
+                spread(h, [])
+            for h in range(chunks):
+                serve(h)
+                if h + ahead < chunks:
+                    send_tokens(h + ahead)
+
+        @pl.when(jnp.logical_not(last))
+        def _():
+            for h in range(chunks):
+                if h < chunks - 1:
+                    serve(h)
+                spread(h, kv_tiles)
+            serve(chunks - 1)
+
+        queries(0)
+    else:
+        for h in range(chunks):
+            serve(h)
+            if h + ahead < chunks:
+                send_tokens(h + ahead)
+            if h >= 1:
+                spread(h - 1, kv_tiles)
+        spread(chunks - 1, kv_tiles)
+        queries(0)
 
     for k in range(1, steps + 1):
 
@@ -359,12 +398,9 @@
     cols = qkv_weight.shape[1]
     steps = devices // 4
     chunks = 4
-    ahead = 3
+    ahead = 2
     col_tile = 256 if cols % 256 == 0 else cols
     tiles = cols // col_tile
-    half = HEAD_SIZE // 2
-    freq = 500000.0 ** (-np.arange(half, dtype=np.float64) * 2.0 / HEAD_SIZE)
-    freq = np.tile(freq.astype(np.float32), PAIR // half)[None]
     pieces_shape = (parts, rows, cols) if cols % 128 else (1, 16, 128)
     return pl.pallas_call(
         functools.partial(kernel, parts, devices, steps, chunks, ahead, col_tile),
@@ -372,7 +408,6 @@
         in_specs=[
             pl.BlockSpec(memory_space=pl.ANY),
             pl.BlockSpec(memory_space=pl.ANY),
-            pl.BlockSpec(memory_space=pltpu.VMEM),
             pl.BlockSpec(memory_space=pltpu.SMEM),
             pl.BlockSpec(memory_space=pltpu.SMEM),
         ],
@@ -402,7 +437,7 @@
         compiler_params=pltpu.CompilerParams(
             collective_id=0, has_side_effects=True, vmem_limit_bytes=62 * 1024 * 1024
         ),
-    )(tokens, qkv_weight, jnp.asarray(freq), doc_lengths, span_order)
+    )(tokens, qkv_weight, doc_lengths, span_order)
 
 
 def solution(mesh):

time: 31.3 us -> 30.9 us (0.987)
  Pallas kernels: 29.4 us -> 29 us
    pallas_call x1, Pallas kernels: 29.4 us -> 29 us  [body(): pl.pallas_call(functools.partial(kernel, parts, devices, steps, chunks, a...]
where the time goes in v3:
time: 30.9 us; the launch traced here: 30.7 us
  Pallas kernels  29 us (94%)
  local copies, waits for them, and re-layouts  1.67 us (5%)
    pallas_call x1, Pallas kernels, body(): pl.pallas_call(functools.partial(kernel, parts, devices, steps, chunks, a...  29 us
    unnamed x1, local copies, waits for them, and re-layouts  1.67 us

profile of v3, /device:TPU:0, one launch (start us, length us, event | category | flops | bytes accessed | tf_op | source)
XLA Modules:
  0.0 30.7 jit_solution(16968374469270283033)
XLA Ops:
  0.0 29.0 %shard_map.46 = bf16[1,128,1024]{2,1,0:T(8,128)(2,1)} custom-call(bf16[1,128,2048]{2,1,0:T(8,128)(2,1)} %tok_ref.1, bf16[2048,768]{1,0:T(8,128)(2,1)} %w_ref.1, s32[1,12]{1,0:T(1,128)} %len_ref.1, s32[1,32]{1,0:T(1,128)} %order_ref.1), custom_call_target="tpu_custom_call" | custom-call | tf_op jit(solution)/shard_map/pallas_call | solution.py:405
  29.0 1.7 %copy.6 = bf16[1,128,1024]{2,1,0:T(8,128)(2,1)} copy(bf16[1,128,1024]{2,1,0:T(8,128)(2,1)} %shard_map.46) | data formatting | bytes 524288
